TPU v7x, 256 devices: a whole 4x4x8 slice. The times are simulated.
256 devices in a mesh: dp: 32 (over z, x), fsdp: 8 (over y, core).
Axes of the slice: x: 4, y: 4, z: 8, core: 2. Of those that a mesh axis runs over, the one named last changes fastest.
Arguments:
- tokens: bfloat16 [4096, 8192], P('dp', 'fsdp'), may hold values from -170 to 170
- out_grad: bfloat16 [4096, 28672], P('dp'), may hold values from -0.25 to 0.25
- sketch_matrix: bfloat16 [4096, 256], P('dp'), may hold values from -4 to 4
- memory: bfloat16 [8192, 1024], P('fsdp'), may hold values from -1.5 to 1.5, as said below
Outputs:
- projected: bfloat16 [8192, 28672], P('fsdp', 'dp')
- new_basis: bfloat16 [8192, 256], P('fsdp')
Inputs may be any that keep to these rules, and one draw needn't show every extreme that they name: memory's columns are orthonormal up to the bfloat16 rounding, scaled by sqrt(8192).
All inputs are finite; a program needn't handle non-finite values.
Results may differ from a plain program's by a relative error of at most 0.0062.
Values may be sent and summed in bfloat16 or wider, within the bound.
No kernel may reach another device: no remote copies, remote signals or barrier semaphores. Data moves between devices by JAX's collectives and lax.ppermute only.
A program may use at most 128 MiB of HBM per device.

v0:
```python
import math

import jax
import jax.numpy as jnp
from jax import lax
from jax.sharding import PartitionSpec as P

D = 8192


def contract_rows(left, right):
    return lax.dot_general(
        left, right, (((0,), (0,)), ((), ())), preferred_element_type=jnp.float32
    )


def contract_exact(left, right):
    return lax.dot_general(
        left,
        right,
        (((0,), (0,)), ((), ())),
        precision=lax.Precision.HIGHEST,
        preferred_element_type=jnp.float32,
    )


def local(tokens, out_grad, sketch_matrix, memory):
    columns = lax.all_to_all(out_grad, "dp", split_axis=1, concat_axis=0, tiled=True)
    gradient = contract_rows(lax.all_gather(tokens, "dp", axis=0, tiled=True), columns)
    partial_sketch = contract_rows(tokens, sketch_matrix)
    sketch = lax.psum(partial_sketch, "dp").astype(jnp.bfloat16)
    sketch = lax.optimization_barrier(sketch)
    coef_first = lax.psum(contract_rows(memory, sketch), "fsdp")
    scaled_first = (coef_first / D).astype(jnp.bfloat16)
    first = sketch.astype(jnp.float32) - jnp.dot(
        memory, scaled_first, preferred_element_type=jnp.float32
    )
    grad_round = lax.optimization_barrier(gradient.astype(jnp.bfloat16))
    grad_wide = grad_round.astype(jnp.float32)
    memory_part = contract_rows(memory, grad_round)
    gram = lax.psum(contract_exact(first, first), "fsdp")
    factor = jnp.linalg.cholesky(gram)
    basis = lax.linalg.triangular_solve(
        factor, first, left_side=False, lower=True, transpose_a=True
    )
    basis_part = contract_exact(basis, grad_wide)
    coef_memory, coef_basis = lax.psum((memory_part, basis_part), "fsdp")
    scaled_memory = (coef_memory / D).astype(jnp.bfloat16)
    correction = jnp.dot(memory, scaled_memory, preferred_element_type=jnp.float32)
    correction = correction + jnp.dot(basis, coef_basis, precision=lax.Precision.HIGHEST)
    projected = (grad_wide - correction).astype(jnp.bfloat16)
    new_basis = (math.sqrt(D) * basis).astype(jnp.bfloat16)
    return (projected, new_basis)


def solution(mesh):
    in_specs = (P("dp", "fsdp"), P("dp", None), P("dp", None), P("fsdp", None))
    out_specs = (P("fsdp", "dp"), P("fsdp", None))
    return jax.shard_map(local, mesh=mesh, in_specs=in_specs, out_specs=out_specs, check_vma=False)
```

profile of v0, /device:TPU:2, one launch (start us, length us, event | category | flops | bytes accessed | tf_op | source)
XLA Modules:
  0.0 596.5 jit_solution(17644260199605330206)
XLA Ops:
  8.0 0.0 copy-start
  8.0 0.0 all-reduce.7.cloned.1.call-start
  8.1 2.4 fusion.20
  10.4 152.2 %all-reduce.12 = bf16[1024,256]{1,0:T(8,128)(2,1)S(1)} all-reduce(f32[1024,256]{1,0:T(8,128)} %fusion.20), channel_id=1, replica_groups=mesh['dp'=32,'fsdp'=8] {'dp'}, use_global_device_ids=true, to_apply=%region_1.0 | all-reduce | flops 262144 | bytes 1572864 | tf_op jit(solution)/shard_map/psum | solution.py:31
  162.6 1.7 convolution_bitcast_fusion.2
  164.3 0.0 all-reduce.7.cloned.1.call-update
  164.4 0.0 all-reduce.9.cloned.1.call-start
  164.4 67.5 %all-reduce.7.cloned.1.call-done = f32[1024,256]{0,1:T(8,128)} async-done(((f32[1024,256]{0,1:T(8,128)}), f32[1024,256]{0,1:T(8,128)}) %all-reduce.7.cloned.1.call-update) | async-done | bytes 1048592 | tf_op jit(solution)/shard_map/psum | solution.py:33
  231.9 2.1 fusion.4
  234.0 2.5 fusion.21
  236.5 0.0 all-reduce.9.cloned.1.call-update
  236.5 0.0 all-gather.2.cloned.1.call-start
  236.6 0.5 all-gather.2.cloned.1.call-update
  237.1 10.4 %copy.16 = bf16[128,28672]{0,1:T(8,128)(2,1)} copy(bf16[128,28672]{1,0:T(8,128)(2,1)} %param.5) | data formatting | bytes 14680064 | tf_op args[1]
  247.5 10.2 %all-to-all-start = ((bf16[128,32,896]{0,2,1:T(8,128)(2,1)}), bf16[128,32,896]{0,2,1:T(8,128)(2,1)}, u32[]{:S(2)}, u32[]{:S(2)}) async-start(bf16[128,32,896]{0,2,1:T(8,128)(2,1)} %bitcast.62), calls=%async_computation | async-start | bytes 14680064 | tf_op jit(solution)/shard_map/all_to_all | solution.py:28
  257.7 0.2 all-reduce.11.cloned.1.call-start
  257.9 44.6 %all-reduce.9.cloned.1.call-done = f32[256,256]{0,1:T(8,128)} async-done(((f32[256,256]{0,1:T(8,128)}), f32[256,256]{0,1:T(8,128)}) %all-reduce.9.cloned.1.call-update) | async-done | bytes 262160 | tf_op jit(solution)/shard_map/psum | solution.py:41
  302.5 1.1 copy.21
  303.6 1.0 fusion.9
  304.6 0.7 copy-done.8
  305.3 11.7 %cholesky.50 = f32[128,128]{1,0:T(8,128)S(1)} custom-call(f32[128,128]{1,0:T(8,128)S(1)} %cholesky.118), custom_call_target="Cholesky" | custom-call | tf_op jit(solution)/shard_map/jit(cholesky)/cholesky | solution.py:42
  317.1 9.8 %custom-call.14 = f32[1,128,128]{1,2,0:T(8,128)S(1)} custom-call(f32[1,128,128]{2,1,0:T(8,128)S(1)} %get-tuple-element.31), custom_call_target="InvertDiagBlocksLowerTriangular" | custom-call | tf_op jit(solution)/shard_map/jit(cholesky)/cholesky | solution.py:42
  326.9 1.0 constant_dynamic-update-slice_fusion.1
  327.9 1.1 convolution_subtract_fusion.1
  329.1 11.7 %cholesky.105 = f32[128,128]{1,0:T(8,128)S(1)} custom-call(f32[128,128]{1,0:T(8,128)S(1)} %convolution_subtract_fusion.1), custom_call_target="Cholesky" | custom-call | tf_op jit(solution)/shard_map/jit(cholesky)/cholesky | solution.py:42
  340.8 0.7 compare_reduce_fusion
  342.7 1.0 select_select_fusion
  343.7 0.1 triangular_solve.58
  343.7 5.4 while.1
  343.9 0.6 fusion.41
  344.5 2.0 bitcast_dynamic-update-slice_fusion.2
  346.5 0.6 fusion.41
  347.1 2.0 bitcast_dynamic-update-slice_fusion.2
  349.1 20.5 %custom-call.15 = f32[2,128,128]{1,2,0:T(8,128)S(1)} custom-call(f32[2,128,128]{2,1,0:T(8,128)} %get-tuple-element.9), custom_call_target="InvertDiagBlocksLowerTriangular" | custom-call | tf_op jit(solution)/shard_map/triangular_solve | solution.py:43
  369.6 0.6 fusion.6
  370.2 1.0 convolution_subtract_fusion
  371.3 0.6 fusion.10
  371.9 91.6 %all-to-all-done = bf16[128,32,896]{0,2,1:T(8,128)(2,1)} async-done(((bf16[128,32,896]{0,2,1:T(8,128)(2,1)}), bf16[128,32,896]{0,2,1:T(8,128)(2,1)}, u32[]{:S(2)}, u32[]{:S(2)}) %all-to-all-start) | async-done | bytes 7340064 | tf_op jit(solution)/shard_map/all_to_all | solution.py:28
  463.5 10.7 %copy.17 = bf16[32,128,896]{2,1,0:T(8,128)(2,1)} copy(bf16[32,128,896]{1,2,0:T(8,128)(2,1)} %bitcast.1) | data formatting | bytes 14680064 | tf_op jit(solution)/shard_map/all_to_all | solution.py:28
  474.2 13.7 %convolution_convert_fusion = bf16[1024,896]{1,0:T(8,128)(2,1)S(1)} fusion(bf16[4096,1024]{1,0:T(8,128)(2,1)} %all-gather.2.cloned.1.call-done, bf16[4096,896]{1,0:T(8,128)(2,1)} %bitcast.63), kind=kOutput, calls=%fused_computation.9 | convolution fusion | flops 7517110272 | bytes 17563648 | tf_op jit(solution)/shard_map/dot_general | solution.py:12
  487.9 4.0 convolution_bitcast_fusion
  491.9 2.9 fusion.5
  494.7 0.0 all-reduce.11.cloned.1.call-update
  494.8 0.9 multiply_convert_fusion.2
  495.7 2.0 copy.22
  497.7 82.0 %all-reduce.11.cloned.1.call-done = (f32[1024,896]{0,1:T(8,128)}, f32[256,896]{1,0:T(8,128)}) async-done(((f32[1024,896]{0,1:T(8,128)}, f32[256,896]{1,0:T(8,128)}), (f32[1024,896]{0,1:T(8,128)}, f32[256,896]{1,0:T(8,128)})) %all-reduce.11.cloned.1.call-update) | async-done | bytes 4587536 | tf_op jit(solution)/shard_map/psum | solution.py:47
  579.8 4.6 fusion.2
  584.3 5.0 fusion.1
  (25 shorter events, 0.2 us)
Async XLA Ops:
  8.0 154.6 %copy-start = (bf16[1024,1024]{1,0:T(8,128)(2,1)S(1)}, bf16[1024,1024]{1,0:T(8,128)(2,1)}, u32[]{:S(2)}) copy-start(bf16[1024,1024]{1,0:T(8,128)(2,1)} %param.7) | copy-start | bytes 6291460
  8.0 223.9 %all-reduce.7.cloned.1.call-start = ((), (), s32[]{:S(2)}) async-start(), calls=%async_computation.2 | async-start | bytes 2097152 | tf_op jit(solution)/shard_map/psum | solution.py:33
  162.6 1.8 copy-start.5
  164.4 138.2 %all-reduce.9.cloned.1.call-start = ((), (), s32[]{:S(2)}) async-start(), calls=%async_computation.3 | async-start | bytes 524288 | tf_op jit(solution)/shard_map/psum | solution.py:41
  236.5 237.7 %all-gather.2.cloned.1.call-start = ((), (), s32[]{:S(2)}) async-start(), calls=%async_computation.1 | async-start | bytes 8650752 | tf_op jit(solution)/shard_map/all_gather | solution.py:29
  247.5 216.1 %all-to-all-start = ((bf16[128,32,896]{0,2,1:T(8,128)(2,1)}), bf16[128,32,896]{0,2,1:T(8,128)(2,1)}, u32[]{:S(2)}, u32[]{:S(2)}) async-start(bf16[128,32,896]{0,2,1:T(8,128)(2,1)} %bitcast.62), calls=%async_computation | async-start | bytes 14680064 | tf_op jit(solution)/shard_map/all_to_all | solution.py:28
  257.7 322.1 %all-reduce.11.cloned.1.call-start = ((), (), s32[]{:S(2)}) async-start(), calls=%async_computation.4 | async-start | bytes 9175040 | tf_op jit(solution)/shard_map/psum | solution.py:47
  304.6 0.7 copy-start.8
  340.8 1.9 copy-start.6
  370.2 1.0 copy-start.1
  487.9 4.0 copy-start.3
  487.9 4.0 copy-start.2
  579.7 4.6 copy-start.4
  579.8 4.6 copy-start.7
Sparse Core Ops, SparseCore 0:
  164.5 67.3 all-reduce.6
  236.6 65.8 all-reduce.8
  494.9 84.8 all-reduce.10
Sparse Core Ops, SparseCore 1:
  239.9 215.0 all-gather.1
where the time goes:
time: 598 us; the launch traced here: 596 us
  waiting for transfers between devices  286 us (48%)
  blocking collectives  152 us (25%)
  other arithmetic  57.3 us (10%)
  matrix products  43.2 us (7%)
  local copies, waits for them, and re-layouts  30.2 us (5%)
  between operations  16.6 us (3%)
  starting transfers between devices  10.5 us (2%)
    psum x1, blocking collectives, local(): sketch = lax.psum(partial_sketch, 'dp').astype(jnp.bfloat16)  152 us
    all_to_all x1, waiting for transfers between devices, local(): lax.all_to_all(out_grad, 'dp', split_axis=1, concat_axis=0, tiled=True)  91.6 us
    psum x1, waiting for transfers between devices, local(): coef_memory, coef_basis = lax.psum((memory_part, basis_part), 'fsdp')  82 us
    psum x1, waiting for transfers between devices, local(): coef_first = lax.psum(contract_rows(memory, sketch), 'fsdp')  67.5 us
    psum x1, waiting for transfers between devices, local(): gram = lax.psum(contract_exact(first, first), 'fsdp')  44.6 us
    another operation x6, other arithmetic, local(): factor = jnp.linalg.cholesky(gram)  34 us
    dot_general x4, matrix products, contract_rows(): lax.dot_general(left, right, (((0,), (0,)), ((), ())), preferred_element_...  21.7 us
    another operation x3, other arithmetic, local(): lax.linalg.triangular_solve(factor, first, left_side=False, lower=True, t...  21.5 us
  transfers between devices with their start and end apart: 5, of which 4 were waited for; matrix products, arithmetic and copies ran while one was open for 15% of the time, Pallas kernels for 0%

commit v1 on v0

v1 whole, which is shorter than its diff:
```python
import math

import jax
import jax.numpy as jnp
from jax import lax
from jax.sharding import PartitionSpec as P

D = 8192
DP, FS = 32, 8
BF, F32 = jnp.bfloat16, jnp.float32
HIGH = lax.Precision.HIGHEST


def contract_rows(left, right, precision=None):
    return lax.dot_general(
        left, right, (((0,), (0,)), ((), ())), precision=precision, preferred_element_type=F32
    )


def swap(x, axis):
    return lax.all_to_all(x, axis, split_axis=0, concat_axis=0, tiled=True)


def sum_scatter(x, axis, n):
    rows = x.shape[0] // n
    return jnp.sum(swap(x, axis).reshape(n, rows, x.shape[1]), axis=0)


def spread(x, axis, n):
    wide = jnp.broadcast_to(x[None], (n,) + x.shape).reshape(n * x.shape[0], x.shape[1])
    return swap(lax.optimization_barrier(wide), axis)


def local(tokens, out_grad, sketch_matrix, memory):
    f = lax.axis_index("fsdp")
    cols = out_grad.shape[1] // DP
    rows = tokens.shape[0] // FS
    token_part = jnp.dot(tokens, memory, preferred_element_type=F32)
    token_own = sum_scatter(token_part, "fsdp", FS)
    token_own = (token_own / D).astype(BF)
    token_coef = spread(token_own, "fsdp", FS)
    clean = tokens.astype(F32) - lax.dot_general(
        token_coef, memory, (((1,), (1,)), ((), ())), preferred_element_type=F32
    )
    clean = clean.astype(BF)
    clean_all = lax.all_gather(clean, "dp", axis=0, tiled=True)
    own = lax.dynamic_slice_in_dim(out_grad, f * rows, rows, 0)
    own = jnp.transpose(own.reshape(rows, DP, cols), (1, 0, 2))
    sk = lax.dynamic_slice_in_dim(sketch_matrix, f * rows, rows, 0)
    own = jnp.concatenate([own, jnp.broadcast_to(sk[None], (DP,) + sk.shape)], axis=2)
    part = swap(own, "dp")
    right = lax.all_gather(part, "fsdp", axis=0, tiled=False)
    right = jnp.transpose(right, (1, 0, 2, 3)).reshape(DP * FS * rows, -1)
    mine = lax.dynamic_slice_in_dim(token_coef, f * 128, 128, 1)
    coef = contract_rows(mine, sketch_matrix)
    coef = jnp.pad(coef.reshape(DP, 4, -1), ((0, 0), (0, 4), (0, 0))).reshape(DP * 8, -1)
    coef = sum_scatter(coef, "dp", DP)
    coef = spread(coef, "dp", DP).reshape(DP, 8, -1)[:, :4].reshape(DP * 4, -1)
    coef = lax.all_gather(coef, "fsdp", axis=0, tiled=True)
    both = contract_rows(clean_all, right)
    gradient, first = both[:, :cols], both[:, cols:]
    gram = contract_rows(first, first, HIGH)
    gram = spread(sum_scatter(gram, "fsdp", FS), "fsdp", FS)
    sketch = first + jnp.dot(memory, coef.astype(BF), preferred_element_type=F32)
    weight = contract_rows(sketch, gradient, HIGH)
    weight = spread(sum_scatter(weight, "fsdp", FS), "fsdp", FS)
    factor = jnp.linalg.cholesky(gram)
    inverse = lax.linalg.triangular_solve(
        factor, jnp.eye(factor.shape[0], dtype=F32), left_side=True, lower=True
    )
    basis = lax.dot_general(first, inverse, (((1,), (1,)), ((), ())), precision=HIGH)
    coef_basis = jnp.dot(inverse, weight, precision=HIGH)
    projected = (gradient - jnp.dot(basis, coef_basis, precision=HIGH)).astype(BF)
    new_basis = (math.sqrt(D) * basis).astype(BF)
    return (projected, new_basis)


def solution(mesh):
    in_specs = (P("dp", "fsdp"), P("dp", None), P("dp", None), P("fsdp", None))
    out_specs = (P("fsdp", "dp"), P("fsdp", None))
    return jax.shard_map(local, mesh=mesh, in_specs=in_specs, out_specs=out_specs, check_vma=False)
```

time: 598 us -> 362 us (0.61)
  waiting for transfers between devices: 286 us -> 91.9 us
  blocking collectives: 152 us -> 104 us
  starting transfers between devices: 10.5 us -> 22.3 us
  local copies, waits for them, and re-layouts: 30.2 us -> 22 us
    psum x3 -> x0, waiting for transfers between devices: 194 us -> none  [the longest x1 82 us: local(): coef_memory, coef_basis = lax.psum((memory_part, basis_part), 'fsdp')]
    psum x1 -> x0, blocking collectives: 152 us -> none  [local(): sketch = lax.psum(partial_sketch, 'dp').astype(jnp.bfloat16)]
    all_to_all x0 -> x4, blocking collectives: none -> 89.5 us  [swap(): return lax.all_to_all(x, axis, split_axis=0, concat_axis=0, tiled=True)]
    all_gather x1 -> x2, waiting for transfers between devices: 0.01 us -> 69.2 us  [the longest x1 69.2 us: local(): clean_all = lax.all_gather(clean, 'dp', axis=0, tiled=True)]
    all_to_all x1 -> x5, waiting for transfers between devices: 91.6 us -> 22.7 us  [swap(): return lax.all_to_all(x, axis, split_axis=0, concat_axis=0, tiled=True)]
    all_gather x0 -> x1, blocking collectives: none -> 14.4 us  [local(): coef = lax.all_gather(coef, 'fsdp', axis=0, tiled=True)]
    all_to_all x1 -> x5, starting transfers between devices: 10.2 us -> 22.2 us  [swap(): return lax.all_to_all(x, axis, split_axis=0, concat_axis=0, tiled=True)]
    unnamed x20 -> x11, local copies, waits for them, and re-layouts: 13.1 us -> 2.93 us
  transfers between devices with their start and end apart: 5 -> 7, of which waited for: 4 -> 5; matrix products, arithmetic and copies ran while one was open for 15% -> 26% of each run, Pallas kernels for 0% -> 0%
where the time goes in v1:
time: 362 us; the launch traced here: 358 us
  blocking collectives  104 us (29%)
  waiting for transfers between devices  91.9 us (25%)
  other arithmetic  57 us (16%)
  matrix products  45.8 us (13%)
  starting transfers between devices  22.3 us (6%)
  local copies, waits for them, and re-layouts  22 us (6%)
  between operations  15.6 us (4%)
    all_to_all x4, blocking collectives, swap(): return lax.all_to_all(x, axis, split_axis=0, concat_axis=0, tiled=True)  89.5 us
    all_gather x1, waiting for transfers between devices, local(): clean_all = lax.all_gather(clean, 'dp', axis=0, tiled=True)  69.2 us
    another operation x6, other arithmetic, local(): factor = jnp.linalg.cholesky(gram)  34 us
    dot_general x4, matrix products, contract_rows(): lax.dot_general(left, right, (((0,), (0,)), ((), ())), precision=precisio...  24.9 us
    all_to_all x5, waiting for transfers between devices, swap(): return lax.all_to_all(x, axis, split_axis=0, concat_axis=0, tiled=True)  22.7 us
    all_to_all x5, starting transfers between devices, swap(): return lax.all_to_all(x, axis, split_axis=0, concat_axis=0, tiled=True)  22.2 us
    another operation x3, other arithmetic, local(): lax.linalg.triangular_solve(factor, jnp.eye(factor.shape[0], dtype=F32),...  21.1 us
    all_gather x1, blocking collectives, local(): coef = lax.all_gather(coef, 'fsdp', axis=0, tiled=True)  14.4 us
  transfers between devices with their start and end apart: 7, of which 5 were waited for; matrix products, arithmetic and copies ran while one was open for 26% of the time, Pallas kernels for 0%

profile of v1, /device:TPU:2, one launch (start us, length us, event | category | flops | bytes accessed | tf_op | source)
XLA Modules:
  0.0 358.4 jit_solution(16808928440042194396)
XLA Ops:
  7.2 1.4 constant_dynamic-slice_fusion.2
  9.3 42.6 %all_to_all.83 = bf16[32,16,1152]{2,1,0:T(8,128)(2,1)} all-to-all(bf16[32,16,1152]{2,1,0:T(8,128)(2,1)S(1)} %copy.19), channel_id=1, replica_groups=mesh['dp'=32,'fsdp'=8] {'dp'}, dimensions={0} | all-to-all | bytes 2359296 | tf_op jit(solution)/shard_map/all_to_all | solution.py:21
  52.4 16.2 %all_to_all.84 = f32[8,16,1024]{2,1,0:T(8,128)S(1)} all-to-all(f32[8,16,1024]{2,1,0:T(8,128)S(1)} %bitcast.78), channel_id=1, replica_groups=mesh['dp'=32,'fsdp'=8] {'fsdp'}, dimensions={0} | all-to-all | bytes 1048576 | tf_op jit(solution)/shard_map/all_to_all | solution.py:21
  68.7 13.1 %all_to_all.85 = bf16[8,16,1024]{2,1,0:T(8,128)(2,1)S(1)} all-to-all(bf16[8,16,1024]{2,1,0:T(8,128)(2,1)S(1)} %broadcast_in_dim.11), channel_id=1, replica_groups=mesh['dp'=32,'fsdp'=8] {'fsdp'}, dimensions={0} | all-to-all | bytes 524288 | tf_op jit(solution)/shard_map/all_to_all | solution.py:21
  81.8 1.5 fusion.3
  83.6 17.6 %all_to_all.86 = f32[32,8,256]{2,1,0:T(8,128)S(1)} all-to-all(f32[32,8,256]{2,1,0:T(8,128)S(1)} %pad.5), channel_id=1, replica_groups=mesh['dp'=32,'fsdp'=8] {'dp'}, dimensions={0} | all-to-all | bytes 524288 | tf_op jit(solution)/shard_map/all_to_all | solution.py:21
  101.3 0.7 broadcast_bitcast_fusion
  101.9 5.7 %all-to-all-start.6 = ((bf16[32,8,256]{2,1,0:T(8,128)(2,1)}), bf16[32,8,256]{2,1,0:T(8,128)(2,1)S(1)}, u32[]{:S(2)}, u32[]{:S(2)}) async-start(bf16[32,8,256]{2,1,0:T(8,128)(2,1)} %bitcast.18), calls=%async_computation.6 | async-start | bytes 262144 | tf_op jit(solution)/shard_map/all_to_all | solution.py:21
  107.6 0.6 iota_compare_fusion
  108.3 8.3 %all-to-all-done.6 = bf16[32,8,256]{2,1,0:T(8,128)(2,1)S(1)} async-done(((bf16[32,8,256]{2,1,0:T(8,128)(2,1)}), bf16[32,8,256]{2,1,0:T(8,128)(2,1)S(1)}, u32[]{:S(2)}, u32[]{:S(2)}) %all-to-all-start.6) | async-done | bytes 131104 | tf_op jit(solution)/shard_map/all_to_all | solution.py:21
  116.6 14.4 %all_gather.15 = bf16[1024,256]{1,0:T(8,128)(2,1)} all-gather(bf16[128,256]{1,0:T(8,128)(2,1)S(1)} %reshape.87), channel_id=1, replica_groups=mesh['dp'=32,'fsdp'=8] {'fsdp'}, dimensions={0}, use_global_device_ids=true | all-gather | bytes 589824 | tf_op jit(solution)/shard_map/all_gather | solution.py:59
  131.0 8.6 %copy.20 = bf16[32,8,16,1152]{3,2,1,0:T(8,128)(2,1)} copy(bf16[32,8,16,1152]{3,2,0,1:T(8,128)(2,1)} %bitcast.72) | data formatting | bytes 18874368 | tf_op jit(solution)/shard_map/transpose | solution.py:53
  139.6 69.2 %all-gather.4.cloned.1.call-done = bf16[4096,1024]{1,0:T(8,128)(2,1)} async-done(((bf16[128,1024]{1,0:T(8,128)(2,1)}), bf16[4096,1024]{1,0:T(8,128)(2,1)}) %all-gather.4.cloned.1.call-update) | async-done | bytes 8388624 | tf_op jit(solution)/shard_map/all_gather | solution.py:46
  208.8 15.5 %fusion.25 = f32[1024,1152]{1,0:T(8,128)S(1)} fusion(bf16[4096,1024]{1,0:T(8,128)(2,1)} %all-gather.4.cloned.1.call-done, bf16[4096,1152]{1,0:T(8,128)(2,1)} %bitcast.73), kind=kOutput, calls=%fused_computation.55 | convolution fusion | flops 9663676416 | bytes 22544384 | tf_op jit(solution)/shard_map/dot_general | solution.py:15
  224.3 2.1 copy-done.1
  226.4 2.6 fusion.6
  229.1 4.3 %all-to-all-start.3 = ((f32[8,32,256]{2,1,0:T(8,128)}), f32[8,32,256]{2,1,0:T(8,128)S(1)}, u32[]{:S(2)}, u32[]{:S(2)}) async-start(f32[8,32,256]{2,1,0:T(8,128)} %bitcast.8), calls=%async_computation.3 | async-start | bytes 524288 | tf_op jit(solution)/shard_map/all_to_all | solution.py:21
  233.4 2.1 fusion.2
  235.5 5.4 %all-to-all-done.3 = f32[8,32,256]{2,1,0:T(8,128)S(1)} async-done(((f32[8,32,256]{2,1,0:T(8,128)}), f32[8,32,256]{2,1,0:T(8,128)S(1)}, u32[]{:S(2)}, u32[]{:S(2)}) %all-to-all-start.3) | async-done | bytes 262176 | tf_op jit(solution)/shard_map/all_to_all | solution.py:21
  240.9 0.7 broadcast_in_dim.13
  241.6 3.6 %all-to-all-start.4 = ((f32[8,32,256]{2,1,0:T(8,128)}), f32[8,32,256]{2,1,0:T(8,128)S(1)}, u32[]{:S(2)}, u32[]{:S(2)}) async-start(f32[8,32,256]{2,1,0:T(8,128)} %broadcast_in_dim.13), calls=%async_computation.4 | async-start | bytes 524288 | tf_op jit(solution)/shard_map/all_to_all | solution.py:21
  245.3 6.6 %fusion = f32[256,896]{1,0:T(8,128)} fusion(f32[1024,256]{1,0:T(8,128)S(1)} %fusion.2, f32[1024,1152]{1,0:T(8,128)} %copy-done.1), kind=kOutput, calls=%fused_computation.3 | convolution fusion | flops 2818572288 | bytes 5636096 | tf_op jit(solution)/shard_map/dot_general | solution.py:15
  251.9 0.7 all-to-all-done.4
  252.5 3.8 %all-to-all-start.7 = ((f32[8,32,896]{2,1,0:T(8,128)}), f32[8,32,896]{2,1,0:T(8,128)S(1)}, u32[]{:S(2)}, u32[]{:S(2)}) async-start(f32[8,32,896]{2,1,0:T(8,128)} %bitcast.76), calls=%async_computation.7 | async-start | bytes 1835008 | tf_op jit(solution)/shard_map/all_to_all | solution.py:21
  256.4 0.8 copy.21
  257.2 1.0 fusion.9
  258.2 0.7 copy-done.3
  258.9 11.7 %cholesky.50 = f32[128,128]{1,0:T(8,128)S(1)} custom-call(f32[128,128]{1,0:T(8,128)S(1)} %cholesky.118), custom_call_target="Cholesky" | custom-call | tf_op jit(solution)/shard_map/jit(cholesky)/cholesky | solution.py:67
  270.7 9.8 %custom-call.14 = f32[1,128,128]{1,2,0:T(8,128)S(1)} custom-call(f32[1,128,128]{2,1,0:T(8,128)S(1)} %get-tuple-element.23), custom_call_target="InvertDiagBlocksLowerTriangular" | custom-call | tf_op jit(solution)/shard_map/jit(cholesky)/cholesky | solution.py:67
  280.5 1.0 constant_dynamic-update-slice_fusion
  281.5 1.1 convolution_subtract_fusion.2
  282.6 11.7 %cholesky.105 = f32[128,128]{1,0:T(8,128)S(1)} custom-call(f32[128,128]{1,0:T(8,128)S(1)} %convolution_subtract_fusion.2), custom_call_target="Cholesky" | custom-call | tf_op jit(solution)/shard_map/jit(cholesky)/cholesky | solution.py:67
  294.4 0.7 compare_reduce_fusion
  296.4 5.2 %while.1 = (s32[]{:T(128)}, f32[256,256]{1,0:T(8,128)S(1)}, s32[2,2]{1,0:T(2,128)S(1)}, f32[2,128,128]{2,1,0:T(8,128)}, s32[]{:T(128)}) while((s32[]{:T(128)}, f32[256,256]{1,0:T(8,128)S(1)}, s32[2,2]{1,0:T(2,128)S(1)}, f32[2,128,128]{2,1,0:T(8,128)}, s32[]{:T(128)}) %tuple.28), condition=%wide.while_cond, body=%wide.while_body.sunk | while | flops 2 | bytes 132705 | solution.py:68
  296.4 0.6 fusion.44
  297.0 2.0 bitcast_dynamic-update-slice_fusion.2
  299.0 0.6 fusion.44
  299.6 2.0 bitcast_dynamic-update-slice_fusion.2
  301.6 21.1 %custom-call.15 = f32[2,128,128]{1,2,0:T(8,128)} custom-call(f32[2,128,128]{2,1,0:T(8,128)} %get-tuple-element.9), custom_call_target="InvertDiagBlocksLowerTriangular" | custom-call | tf_op jit(solution)/shard_map/triangular_solve | solution.py:68
  322.8 1.0 broadcast_in_dim.15
  323.8 4.8 %all-to-all-start.8 = ((f32[8,32,896]{2,1,0:T(8,128)}), f32[8,32,896]{2,1,0:T(8,128)}, u32[]{:S(2)}, u32[]{:S(2)}) async-start(f32[8,32,896]{2,1,0:T(8,128)} %bitcast.22), calls=%async_computation.8 | async-start | bytes 1835008 | tf_op jit(solution)/shard_map/all_to_all | solution.py:21
  328.6 1.1 fusion.11
  329.7 1.0 convolution_subtract_fusion.1
  330.7 1.1 fusion.14
  331.8 3.0 multiply_convert_fusion
  334.9 8.3 %all-to-all-done.8 = f32[8,32,896]{2,1,0:T(8,128)} async-done(((f32[8,32,896]{2,1,0:T(8,128)}), f32[8,32,896]{2,1,0:T(8,128)}, u32[]{:S(2)}, u32[]{:S(2)}) %all-to-all-start.8) | async-done | bytes 917536 | tf_op jit(solution)/shard_map/all_to_all | solution.py:21
  343.2 2.2 fusion.10
  345.4 6.1 %subtract_convert_fusion = bf16[1024,896]{1,0:T(8,128)(2,1)} fusion(f32[1024,1152]{1,0:T(8,128)} %copy-done.1, f32[1024,256]{1,0:T(8,128)S(1)} %get-tuple-element.27, f32[256,896]{1,0:T(8,128)S(1)} %fusion.10), kind=kOutput, calls=%fused_computation.2 | convolution fusion | flops 2820407296 | bytes 7471104 | tf_op jit(solution)/shard_map/dot_general | solution.py:73
  (41 shorter events, 1.9 us)
Async XLA Ops:
  7.2 44.8 %copy-start = (bf16[1024,1024]{1,0:T(8,128)(2,1)S(1)}, bf16[1024,1024]{1,0:T(8,128)(2,1)}, u32[]{:S(2)}) copy-start(bf16[1024,1024]{1,0:T(8,128)(2,1)} %param.7) | copy-start | bytes 6291460
  7.2 1.6 copy-start.4
  7.2 123.8 %all-gather.6.cloned.1.call-start = ((), (), s32[]{:S(2)}) async-start(), calls=%async_computation.10 | async-start | bytes 10616832 | tf_op jit(solution)/shard_map/all_gather | solution.py:52
  8.8 43.2 %copy-start.2 = (bf16[128,1024]{1,0:T(8,128)(2,1)S(1)}, bf16[128,1024]{1,0:T(8,128)(2,1)}, u32[]{:S(2)}) copy-start(bf16[128,1024]{1,0:T(8,128)(2,1)} %param.4) | copy-start | bytes 786436
  51.9 156.8 %all-gather.4.cloned.1.call-start = ((), (), s32[]{:S(2)}) async-start(), calls=%async_computation.9 | async-start | bytes 8650752 | tf_op jit(solution)/shard_map/all_gather | solution.py:46
  101.9 14.6 %all-to-all-start.6 = ((bf16[32,8,256]{2,1,0:T(8,128)(2,1)}), bf16[32,8,256]{2,1,0:T(8,128)(2,1)S(1)}, u32[]{:S(2)}, u32[]{:S(2)}) async-start(bf16[32,8,256]{2,1,0:T(8,128)(2,1)} %bitcast.18), calls=%async_computation.6 | async-start | bytes 262144 | tf_op jit(solution)/shard_map/all_to_all | solution.py:21
  224.3 2.1 copy-start.1
  229.1 11.8 %all-to-all-start.3 = ((f32[8,32,256]{2,1,0:T(8,128)}), f32[8,32,256]{2,1,0:T(8,128)S(1)}, u32[]{:S(2)}, u32[]{:S(2)}) async-start(f32[8,32,256]{2,1,0:T(8,128)} %bitcast.8), calls=%async_computation.3 | async-start | bytes 524288 | tf_op jit(solution)/shard_map/all_to_all | solution.py:21
  241.6 10.9 %all-to-all-start.4 = ((f32[8,32,256]{2,1,0:T(8,128)}), f32[8,32,256]{2,1,0:T(8,128)S(1)}, u32[]{:S(2)}, u32[]{:S(2)}) async-start(f32[8,32,256]{2,1,0:T(8,128)} %broadcast_in_dim.13), calls=%async_computation.4 | async-start | bytes 524288 | tf_op jit(solution)/shard_map/all_to_all | solution.py:21
  252.5 70.2 %all-to-all-start.7 = ((f32[8,32,896]{2,1,0:T(8,128)}), f32[8,32,896]{2,1,0:T(8,128)S(1)}, u32[]{:S(2)}, u32[]{:S(2)}) async-start(f32[8,32,896]{2,1,0:T(8,128)} %bitcast.76), calls=%async_computation.7 | async-start | bytes 1835008 | tf_op jit(solution)/shard_map/all_to_all | solution.py:21
  258.2 0.7 copy-start.3
  323.8 19.5 %all-to-all-start.8 = ((f32[8,32,896]{2,1,0:T(8,128)}), f32[8,32,896]{2,1,0:T(8,128)}, u32[]{:S(2)}, u32[]{:S(2)}) async-start(f32[8,32,896]{2,1,0:T(8,128)} %bitcast.22), calls=%async_computation.8 | async-start | bytes 1835008 | tf_op jit(solution)/shard_map/all_to_all | solution.py:21
Sparse Core Ops, SparseCore 0:
  52.1 57.2 all-gather.5
  112.5 96.1 all-gather.3
